TPU v7x, 256 devices: a whole 4x4x8 slice. The times are simulated.
256 devices in a mesh: query: 32 (over x, z_hi, y), entity: 8 (over z_lo, core).
Axes of the slice: x: 4, y: 4, z: 8 (z_hi: 2, z_lo: 4; z = z_hi * 4 + z_lo), core: 2. Of those that a mesh axis runs over, the one named last changes fastest.
Arguments:
- anchor_ids: int32 [16384], P('query'), may hold values from 0 to 32767
- relation_ids: int32 [16384], P('query'), may hold values from 0 to 4130
- side_flags: int32 [16384], P('query'), may hold values from 0 to 1
- teacher_entities: bfloat16 [32768, 1000], P(('entity', 'query')), may hold values from -1.2 to 1.2, as said below
- student_entities: bfloat16 [32768, 128], P(('entity', 'query')), may hold values from -2.1 to 2.1, as said below
- teacher_relations: bfloat16 [4131, 1000], replicated, may hold values from -9 to 33, as said below
- student_relations: bfloat16 [4131, 128], replicated, may hold values from -9 to 63.6875, as said below
Outputs:
- divergence: float32 [16384], P('query')
- entity_grad: float32 [32768, 128], P(('entity', 'query'))
- query_grad: float32 [16384, 128], P('query')
Inputs may be any that keep to these rules, and one draw needn't show every extreme that they name: `teacher_entities`: Real-valued embeddings. `student_entities`: Real-valued embeddings. `teacher_relations`: Real-valued embeddings. `student_relations`: Real-valued embeddings.
All inputs are finite; a program needn't handle non-finite values.
Results may differ from a plain program's by a relative error of at most 0.013.
Values may be sent and summed in bfloat16 or wider, within the bound.
A program may use at most 128 MiB of HBM per device.

v0:
```python
import jax
import jax.numpy as jnp
from jax import lax
from jax.sharding import PartitionSpec as P


def query_vectors(anchor, relation, flags):
    half = anchor.shape[1] // 2
    sign = (2 * flags - 1).astype(jnp.float32)[:, None]
    a_re = anchor[:, :half]
    a_im = anchor[:, half:]
    r_re = relation[:, :half]
    r_im = relation[:, half:]
    real = a_re * r_re - sign * a_im * r_im
    imag = a_im * r_re + sign * a_re * r_im
    return jnp.concatenate([real, imag], axis=1).astype(jnp.bfloat16)


def per_device(
    anchor_ids,
    relation_ids,
    side_flags,
    teacher_entities,
    student_entities,
    teacher_relations,
    student_relations,
):
    teacher_slab, student_slab = (
        lax.all_gather(teacher_entities, "query", axis=0, tiled=True),
        lax.all_gather(student_entities, "query", axis=0, tiled=True),
    )
    slab = teacher_slab.shape[0]
    offset = lax.axis_index("entity") * slab
    local = anchor_ids - offset
    inside = ((local >= 0) & (local < slab))[:, None]
    safe = jnp.clip(local, 0, slab - 1)
    teacher_part = jnp.where(inside, jnp.take(teacher_slab, safe, axis=0).astype(jnp.float32), 0.0)
    student_part = jnp.where(inside, jnp.take(student_slab, safe, axis=0).astype(jnp.float32), 0.0)
    teacher_anchor, student_anchor = (
        lax.psum(teacher_part.astype(jnp.bfloat16), "entity").astype(jnp.float32),
        lax.psum(student_part.astype(jnp.bfloat16), "entity").astype(jnp.float32),
    )
    query_teacher = query_vectors(
        teacher_anchor,
        jnp.take(teacher_relations, relation_ids, axis=0).astype(jnp.float32),
        side_flags,
    )
    query_student = query_vectors(
        student_anchor,
        jnp.take(student_relations, relation_ids, axis=0).astype(jnp.float32),
        side_flags,
    )
    rows = query_teacher.shape[0]
    block = 1024
    count = slab // block
    teacher_blocks = teacher_slab.reshape(count, block, teacher_slab.shape[1])
    student_blocks = student_slab.reshape(count, block, student_slab.shape[1])

    def first_pass(carry, items):
        top_t, total_t, weighted, top_s, total_s = carry
        t = jnp.dot(query_teacher, items[0].T, preferred_element_type=jnp.float32)
        s = jnp.dot(query_student, items[1].T, preferred_element_type=jnp.float32)
        new_t = jnp.maximum(top_t, jnp.max(t, axis=1))
        factor_t = jnp.exp(top_t - new_t)
        expo_t = jnp.exp(t - new_t[:, None])
        total_t = total_t * factor_t + jnp.sum(expo_t, axis=1)
        weighted = weighted * factor_t + jnp.sum(expo_t * (t - s), axis=1)
        new_s = jnp.maximum(top_s, jnp.max(s, axis=1))
        total_s = total_s * jnp.exp(top_s - new_s) + jnp.sum(jnp.exp(s - new_s[:, None]), axis=1)
        kept = None
        return ((new_t, total_t, weighted, new_s, total_s), kept)

    lowest = jnp.full((rows,), -jnp.inf, jnp.float32)
    nothing = jnp.zeros((rows,), jnp.float32)
    stats, kept = lax.scan(
        first_pass, (lowest, nothing, nothing, lowest, nothing), (teacher_blocks, student_blocks)
    )
    top_t, total_t, weighted, top_s, total_s = stats
    best_t, best_s = lax.pmax((top_t, top_s), "entity")
    factor_t = jnp.exp(top_t - best_t)
    factor_s = jnp.exp(top_s - best_s)
    total_t, weighted, total_s = lax.psum(
        (total_t * factor_t, weighted * factor_t, total_s * factor_s), "entity"
    )
    top_t, top_s = (best_t, best_s)
    divergence = weighted / total_t - top_t - jnp.log(total_t) + top_s + jnp.log(total_s)

    def second_pass(q_grad, items):
        t = jnp.dot(query_teacher, items[0].T, preferred_element_type=jnp.float32)
        s = jnp.dot(query_student, items[1].T, preferred_element_type=jnp.float32)
        prob_t = jnp.exp(t - top_t[:, None]) / total_t[:, None]
        prob_s = jnp.exp(s - top_s[:, None]) / total_s[:, None]
        weights = (prob_s - prob_t).astype(jnp.bfloat16)
        grad_block = jnp.dot(weights.T, query_student, preferred_element_type=jnp.float32)
        q_grad = q_grad + jnp.dot(weights, items[1], preferred_element_type=jnp.float32)
        return (q_grad, grad_block)

    start = jnp.zeros((rows, query_student.shape[1]), jnp.float32)
    q_grad, grad_blocks = lax.scan(second_pass, start, (teacher_blocks, student_blocks))
    slab_grad = grad_blocks.reshape(slab, query_student.shape[1])
    entity_grad = lax.psum_scatter(slab_grad, "query", scatter_dimension=0, tiled=True)
    query_grad = lax.psum(q_grad, "entity")
    return (divergence, entity_grad, query_grad)


def solution(mesh):
    in_specs = (
        P("query"),
        P("query"),
        P("query"),
        P(("entity", "query"), None),
        P(("entity", "query"), None),
        P(),
        P(),
    )
    out_specs = (P("query"), P(("entity", "query"), None), P("query", None))
    return jax.shard_map(
        per_device, mesh=mesh, in_specs=in_specs, out_specs=out_specs, check_vma=False
    )
```

profile of v0, /device:TPU:32, one launch (start us, length us, event | category | flops | bytes accessed | tf_op | source)
XLA Modules:
  0.0 744.2 jit_solution(13715478936245018552)
XLA Ops:
  7.2 0.7 all-gather.5.cloned.1.call-update
  8.0 1.8 copy.10
  9.9 0.7 compare_and_fusion.1
  10.6 83.7 %all-gather.5.cloned.1.call-done = bf16[4096,128]{1,0:T(8,128)(2,1)} async-done(((bf16[128,128]{1,0:T(8,128)(2,1)}), bf16[4096,128]{1,0:T(8,128)(2,1)}) %all-gather.5.cloned.1.call-update) | async-done | bytes 1048592 | tf_op jit(solution)/shard_map/all_gather | solution.py:30
  94.3 2.4 gather_fusion.2
  96.7 0.9 select_convert_fusion.2
  97.5 149.9 %all-gather.3.cloned.1.call-done = bf16[4096,1000]{1,0:T(8,128)(2,1)} async-done(((bf16[128,1000]{1,0:T(8,128)(2,1)}), bf16[4096,1000]{1,0:T(8,128)(2,1)}) %all-gather.3.cloned.1.call-update) | async-done | bytes 8192016 | tf_op jit(solution)/shard_map/all_gather | solution.py:29
  247.4 7.2 gather_fusion
  254.6 1.3 select_convert_fusion
  256.1 12.1 %copy.11 = bf16[4131,1000]{1,0:T(8,128)(2,1)} copy(bf16[4131,1000]{0,1:T(8,128)(2,1)} %param.16) | data formatting | bytes 16524000 | tf_op args[5]
  268.3 8.0 %gather_fusion.1 = bf16[512,1000]{1,0:T(8,128)(2,1)} fusion(bf16[4131,1000]{1,0:T(8,128)(2,1)} %copy.11, s32[1024]{0:T(1024)S(1)} %pad_clamp_fusion), kind=kCustom, calls=%fused_computation.1 | custom fusion | bytes 2050048 | tf_op jit(solution)/shard_map/jit(_take)/gather | solution.py:45
  276.3 1.3 gather_fusion.3
  277.7 0.6 add_convert_fusion.2
  278.3 0.8 select_convert_fusion.3
  279.1 1.4 select_convert_fusion.1
  280.6 43.3 %all-reduce.8.cloned.1.call-done = (bf16[512,1000]{1,0:T(8,128)(2,1)}, bf16[512,128]{1,0:T(8,128)(2,1)}) async-done(((bf16[512,1000]{1,0:T(8,128)(2,1)}, bf16[512,128]{1,0:T(8,128)(2,1)}), (bf16[512,1000]{1,0:T(8,128)(2,1)}, bf16[512,128]{1,0:T(8,128)(2,1)})) %all-reduce.8.cloned.1.call-update) | async-done | bytes 1155088 | tf_op jit(solution)/shard_map/psum | solution.py:40
  323.9 1.5 convert_element_type.33
  325.4 1.0 subtract_convert_fusion.1
  326.4 1.3 pad_maximum_fusion
  328.1 46.0 %while.32 = (s32[]{:T(128)}, f32[512]{0:T(512)S(1)}, f32[512]{0:T(512)}, f32[512]{0:T(512)}, f32[512]{0:T(512)}, /*index=5*/f32[512]{0:T(512)}, bf16[4,1024,1000...) while((s32[]{:T(128)}, f32[512]{0:T(512)S(1)}, ...), condition=%wide.region_8.9_spmd.clone, body=%wide.region_2.8_spmd.clone.sunk | while | flops 1187518464 | bytes 12046677 | solution.py:75
  328.1 5.1 fusion.51
  333.2 2.0 fusion.52
  335.2 0.7 select_maximum_fusion.4
  335.9 0.7 select_maximum_fusion.5
  336.6 2.4 multiply_reduce_fusion.2
  339.0 0.6 copy.31
  339.6 5.1 fusion.51
  344.7 2.0 fusion.52
  346.7 0.7 select_maximum_fusion.4
  347.4 0.7 select_maximum_fusion.5
  348.1 2.4 multiply_reduce_fusion.2
  350.6 0.6 copy.31
  351.2 5.1 fusion.51
  356.2 2.0 fusion.52
  358.2 0.7 select_maximum_fusion.4
  358.9 0.7 select_maximum_fusion.5
  359.6 2.4 multiply_reduce_fusion.2
  362.1 0.6 copy.31
  362.7 5.1 fusion.51
  367.7 2.0 fusion.52
  369.7 0.7 select_maximum_fusion.4
  370.4 0.7 select_maximum_fusion.5
  371.1 2.4 multiply_reduce_fusion.2
  374.2 14.8 %all-reduce.1 = (f32[512]{0:T(512)}, f32[512]{0:T(512)}) all-reduce(f32[512]{0:T(512)} %get-tuple-element.120, f32[512]{0:T(512)S(1)} %get-tuple-element.118), channel_id=1, replica_groups=mesh['query'=32,'entity'=8] {'entity'}, use_global_device_ids=true, to_apply=%region_12.13 | all-reduce | flops 1024 | bytes 8192 | tf_op jit(solution)/shard_map/pmax | solution.py:79
  389.0 0.7 fusion.24
  389.7 14.6 %all-reduce = (f32[512]{0:T(512)S(1)}, f32[512]{0:T(512)}, f32[512]{0:T(512)}) all-reduce(f32[512]{0:T(512)S(1)} %get-tuple-element.261, f32[512]{0:T(512)S(1)} %get-tuple-element.259, f32[512]{0:T(512)S(1)} %get-tuple-element.258), channel_id=1, replica_groups=mesh['query'=32,'entity'=8] {'entity'}, use_global_device_ids=true, to_apply=%region_13.14 | all-reduce | flops 1536 | bytes 12288 | tf_op jit(solution)/shard_map/psum | solution.py:82
  404.3 26.0 %while.33 = (s32[]{:T(128)}, f32[512,128]{1,0:T(8,128)S(1)}, f32[4,1024,128]{2,1,0:T(8,128)}, bf16[4,1024,128]{2,1,0:T(8,128)(2,1)}, bf16[512,128]{1,0:T(8,128)(...) while((s32[]{:T(128)}, f32[512,128]{1,0:T(8,128)S(1)}, ...), condition=%wide.region_15.16_spmd.clone, body=%wide.region_14.15_spmd.clone.sunk | while | flops 1454505984 | bytes 16531671 | solution.py:99
  404.3 3.2 fusion.62
  407.6 1.5 subtract_convert_fusion.4
  409.6 1.2 fusion.63
  410.8 3.2 fusion.62
  414.1 1.5 subtract_convert_fusion.4
  416.1 1.2 fusion.63
  417.3 3.2 fusion.62
  420.6 1.5 subtract_convert_fusion.4
  422.6 1.2 fusion.63
  423.8 3.2 fusion.62
  427.1 1.5 subtract_convert_fusion.4
  429.1 1.2 fusion.63
  430.3 0.7 copy-done.2
  431.6 1.3 log_add_fusion
  432.9 69.5 %all-reduce.6.cloned.1.call-done = f32[512,128]{1,0:T(8,128)} async-done(((f32[512,128]{1,0:T(8,128)}), f32[512,128]{1,0:T(8,128)}) %all-reduce.6.cloned.1.call-update) | async-done | bytes 262160 | tf_op jit(solution)/shard_map/psum | solution.py:102
  502.4 233.6 %reduce-scatter.2.cloned.1.call-done = f32[128,128]{1,0:T(8,128)} async-done(((f32[4096,128]{1,0:T(8,128)}), f32[128,128]{1,0:T(8,128)}) %reduce-scatter.2.cloned.1.call-update) | async-done | bytes 65552 | tf_op jit(solution)/shard_map/reduce_scatter | solution.py:101
  736.0 1.7 copy.43
  (125 shorter events, 4.1 us)
Async XLA Ops:
  7.2 269.1 %copy-start = (bf16[4131,128]{1,0:T(8,128)(2,1)S(1)}, bf16[4131,128]{1,0:T(8,128)(2,1)}, u32[]{:S(2)}) copy-start(bf16[4131,128]{1,0:T(8,128)(2,1)} %param.17) | copy-start | bytes 3172612
  7.2 87.1 %all-gather.5.cloned.1.call-start = ((), (), s32[]{:S(2)}) async-start(), calls=%async_computation.2 | async-start | bytes 1081344 | tf_op jit(solution)/shard_map/all_gather | solution.py:30
  7.9 239.5 %all-gather.3.cloned.1.call-start = ((), (), s32[]{:S(2)}) async-start(), calls=%async_computation.1 | async-start | bytes 8650752 | tf_op jit(solution)/shard_map/all_gather | solution.py:29
  9.8 314.0 %all-reduce.8.cloned.1.call-start = ((), (), s32[]{:S(2)}) async-start(), calls=%async_computation.5 | async-start | bytes 2359296 | tf_op jit(solution)/shard_map/psum | solution.py:40
  254.6 1.4 copy-start.13
  256.0 246.4 %all-reduce.6.cloned.1.call-start = ((), (), s32[]{:S(2)}) async-start(), calls=%async_computation.4 | async-start | bytes 524288 | tf_op jit(solution)/shard_map/psum | solution.py:102
  268.3 9.4 %copy-start.14 = (s32[512]{0:T(512)S(1)}, s32[512]{0:T(512)}, u32[]{:S(2)}) copy-start(s32[512]{0:T(512)} %param.13) | copy-start | bytes 6148
  323.9 1.5 copy-start.5
  323.9 1.5 copy-start.12
  326.4 1.3 copy-start.3
  336.5 2.4 copy-start.4
  336.5 2.4 copy-start.6
  336.5 2.4 copy-start.8
  336.6 2.4 copy-start.10
  339.0 0.6 copy-start.7
  339.0 0.6 copy-start.9
  339.0 0.6 copy-start.11
  348.1 2.4 copy-start.4
  348.1 2.4 copy-start.6
  348.1 2.4 copy-start.8
  348.1 2.4 copy-start.10
  350.5 0.6 copy-start.7
  350.5 0.6 copy-start.9
  350.5 0.6 copy-start.11
  359.6 2.4 copy-start.4
  359.6 2.4 copy-start.6
  359.6 2.4 copy-start.8
  359.6 2.4 copy-start.10
  362.0 0.6 copy-start.7
  362.0 0.6 copy-start.9
  362.0 0.6 copy-start.11
  371.1 2.4 copy-start.4
  371.1 2.4 copy-start.6
  371.1 2.4 copy-start.8
  371.1 2.4 copy-start.10
  373.5 0.6 copy-start.7
  373.5 0.6 copy-start.9
  373.5 0.6 copy-start.11
  404.3 3.2 copy-start.1
  404.3 3.2 copy-start.15
  410.8 3.2 copy-start.1
  410.8 3.2 copy-start.15
  417.3 3.2 copy-start.1
  417.3 3.2 copy-start.15
  423.8 3.2 copy-start.1
  423.8 3.2 copy-start.15
  430.3 0.7 copy-start.2
  430.3 1.3 copy-start.16
  430.3 1.3 copy-start.17
  431.0 305.0 %reduce-scatter.2.cloned.1.call-start = ((), (), s32[]{:S(2)}) async-start(), calls=%async_computation.3 | async-start | bytes 2162688 | tf_op jit(solution)/shard_map/reduce_scatter | solution.py:101
Sparse Core Ops, SparseCore 0:
  11.4 82.7 all-gather.4
  98.4 149.0 all-gather.2
  256.1 67.6 all-reduce.7
  431.1 71.2 all-reduce.5
  505.5 230.4 reduce-scatter.1
where the time goes:
time: 745 us; the launch traced here: 744 us
  waiting for transfers between devices  581 us (78%)
  matrix products  53.9 us (7%)
  local copies, waits for them, and re-layouts  37.8 us (5%)
  blocking collectives  29.4 us (4%)
  other arithmetic  27 us (4%)
  between operations  14 us (2%)
    reduce_scatter x1, waiting for transfers between devices, per_device(): lax.psum_scatter(slab_grad, 'query', scatter_dimension=0, tiled=True)  234 us
    all_gather x1, waiting for transfers between devices, per_device(): lax.all_gather(teacher_entities, 'query', axis=0, tiled=True)  150 us
    all_gather x1, waiting for transfers between devices, per_device(): lax.all_gather(student_entities, 'query', axis=0, tiled=True)  83.7 us
    psum x1, waiting for transfers between devices, per_device(): query_grad = lax.psum(q_grad, 'entity')  69.5 us
    psum x1, waiting for transfers between devices, per_device(): lax.psum(teacher_part.astype(jnp.bfloat16), 'entity').astype(jnp.float32)  43.3 us
    dot_general x4, matrix products, first_pass(): t = jnp.dot(query_teacher, items[0].T, preferred_element_type=jnp.float32)  20.3 us
    unnamed x21, local copies, waits for them, and re-layouts  16.4 us
  transfers between devices with their start and end apart: 5, of which 5 were waited for; matrix products, arithmetic and copies ran while one was open for 4% of the time, Pallas kernels for 0%

commit v1 on v0

--- a/solution.py
+++ b/solution.py
@@ -2,6 +2,13 @@
 import jax.numpy as jnp
 from jax import lax
 from jax.sharding import PartitionSpec as P
+
+frames_wait = lambda matrix: jnp.concatenate(
+    lax.all_to_all(
+        jnp.stack(lax.axis_size("query") * [matrix]), split_axis=0, concat_axis=0, axis_name="query"
+    ),
+    axis=0,
+)
 
 
 def query_vectors(anchor, relation, flags):
@@ -26,7 +33,7 @@
     student_relations,
 ):
     teacher_slab, student_slab = (
-        lax.all_gather(teacher_entities, "query", axis=0, tiled=True),
+        frames_wait(teacher_entities),
         lax.all_gather(student_entities, "query", axis=0, tiled=True),
     )
     slab = teacher_slab.shape[0]

time: 745 us -> 783 us (1.051)
  local copies, waits for them, and re-layouts: 37.8 us -> 52.7 us
  starting transfers between devices: 0.2 us -> 13.6 us
  waiting for transfers between devices: 581 us -> 591 us
    all_gather x1, waiting for transfers between devices: 83.7 us -> 243 us  [per_device(): lax.all_gather(student_entities, 'query', axis=0, tiled=True)]
    all_gather x1 -> x0, waiting for transfers between devices: 150 us -> none  [per_device(): lax.all_gather(teacher_entities, 'query', axis=0, tiled=True)]
    all_to_all x0 -> x1, starting transfers between devices: none -> 13.3 us  [lax.all_to_all(jnp.stack(lax.axis_size('query') * [matrix]), split_axis=0...]
    all_to_all x0 -> x1, local copies, waits for them, and re-layouts: none -> 11.3 us  [lax.all_to_all(jnp.stack(lax.axis_size('query') * [matrix]), split_axis=0...]
    unnamed x21 -> x22, local copies, waits for them, and re-layouts: 16.4 us -> 14.7 us
  transfers between devices with their start and end apart: 5 -> 5, of which waited for: 5 -> 4; matrix products, arithmetic and copies ran while one was open for 4% -> 4% of each run, Pallas kernels for 0% -> 0%
where the time goes in v1:
time: 783 us; the launch traced here: 781 us
  waiting for transfers between devices  591 us (75%)
  matrix products  53.9 us (7%)
  local copies, waits for them, and re-layouts  52.7 us (7%)
  blocking collectives  29.3 us (4%)
  other arithmetic  26.3 us (3%)
  between operations  14 us (2%)
  starting transfers between devices  13.6 us (2%)
    all_gather x1, waiting for transfers between devices, per_device(): lax.all_gather(student_entities, 'query', axis=0, tiled=True)  243 us
    reduce_scatter x1, waiting for transfers between devices, per_device(): lax.psum_scatter(slab_grad, 'query', scatter_dimension=0, tiled=True)  233 us
    psum x1, waiting for transfers between devices, per_device(): query_grad = lax.psum(q_grad, 'entity')  69.6 us
    psum x1, waiting for transfers between devices, per_device(): lax.psum(teacher_part.astype(jnp.bfloat16), 'entity').astype(jnp.float32)  43 us
    dot_general x4, matrix products, first_pass(): t = jnp.dot(query_teacher, items[0].T, preferred_element_type=jnp.float32)  20.3 us
  transfers between devices with their start and end apart: 5, of which 4 were waited for; matrix products, arithmetic and copies ran while one was open for 4% of the time, Pallas kernels for 0%

profile of v1, /device:TPU:32, one launch (start us, length us, event | category | flops | bytes accessed | tf_op | source)
XLA Modules:
  0.0 781.1 jit_solution(3545830057601110933)
XLA Ops:
  7.2 5.2 stack.2
  12.4 13.3 %all-to-all-start = ((bf16[32,128,1000]{1,2,0:T(8,128)(2,1)}), bf16[32,128,1000]{1,2,0:T(8,128)(2,1)}, u32[]{:S(2)}, u32[]{:S(2)}) async-start(bf16[32,128,1000]{1,2,0:T(8,128)(2,1)} %stack.2), calls=%async_computation | async-start | bytes 16384000 | tf_op jit(solution)/shard_map/all_to_all | solution.py:7
  25.8 0.7 all-gather.2.cloned.1.call-update
  26.6 243.5 %all-gather.2.cloned.1.call-done = bf16[4096,128]{1,0:T(8,128)(2,1)} async-done(((bf16[128,128]{1,0:T(8,128)(2,1)}), bf16[4096,128]{1,0:T(8,128)(2,1)}) %all-gather.2.cloned.1.call-update) | async-done | bytes 1048592 | tf_op jit(solution)/shard_map/all_gather | solution.py:37
  270.0 2.4 gather_fusion.2
  272.5 0.9 select_convert_fusion.2
  273.3 11.3 %copy.14 = bf16[32,128,1000]{2,1,0:T(8,128)(2,1)} copy(bf16[32,128,1000]{1,2,0:T(8,128)(2,1)} %all-to-all-done) | data formatting | bytes 16384000 | tf_op jit(solution)/shard_map/all_to_all | solution.py:7
  284.7 7.2 gather_fusion
  291.9 1.3 select_convert_fusion
  293.5 12.3 %copy.16 = bf16[4131,1000]{1,0:T(8,128)(2,1)} copy(bf16[4131,1000]{0,1:T(8,128)(2,1)} %param.16) | data formatting | bytes 16524000 | tf_op args[5]
  305.8 8.0 %gather_fusion.1 = bf16[512,1000]{1,0:T(8,128)(2,1)} fusion(bf16[4131,1000]{1,0:T(8,128)(2,1)} %copy.16, s32[1024]{0:T(1024)S(1)} %pad_clamp_fusion), kind=kCustom, calls=%fused_computation.1 | custom fusion | bytes 2050048 | tf_op jit(solution)/shard_map/jit(_take)/gather | solution.py:52
  313.8 1.3 gather_fusion.3
  315.2 0.6 add_convert_fusion.2
  315.8 0.8 select_convert_fusion.3
  316.6 1.4 select_convert_fusion.1
  318.1 43.0 %all-reduce.8.cloned.1.call-done = (bf16[512,1000]{1,0:T(8,128)(2,1)}, bf16[512,128]{1,0:T(8,128)(2,1)}) async-done(((bf16[512,1000]{1,0:T(8,128)(2,1)}, bf16[512,128]{1,0:T(8,128)(2,1)}), (bf16[512,1000]{1,0:T(8,128)(2,1)}, bf16[512,128]{1,0:T(8,128)(2,1)})) %all-reduce.8.cloned.1.call-update) | async-done | bytes 1155088 | tf_op jit(solution)/shard_map/psum | solution.py:47
  361.1 1.5 convert_element_type.33
  362.6 1.0 subtract_convert_fusion.1
  363.7 1.3 pad_maximum_fusion
  365.4 46.0 %while.32 = (s32[]{:T(128)}, f32[512]{0:T(512)S(1)}, f32[512]{0:T(512)}, f32[512]{0:T(512)}, f32[512]{0:T(512)}, /*index=5*/f32[512]{0:T(512)}, bf16[4,1024,1000...) while((s32[]{:T(128)}, f32[512]{0:T(512)S(1)}, ...), condition=%wide.region_8.9_spmd.clone, body=%wide.region_2.8_spmd.clone.sunk | while | flops 1187518464 | bytes 12046677 | solution.py:82
  365.4 5.1 fusion.51
  370.4 2.0 fusion.52
  372.4 0.7 select_maximum_fusion.4
  373.1 0.7 select_maximum_fusion.5
  373.8 2.4 multiply_reduce_fusion.2
  376.3 0.6 copy.36
  376.9 5.1 fusion.51
  381.9 2.0 fusion.52
  383.9 0.7 select_maximum_fusion.4
  384.6 0.7 select_maximum_fusion.5
  385.3 2.4 multiply_reduce_fusion.2
  387.8 0.6 copy.36
  388.4 5.1 fusion.51
  393.4 2.0 fusion.52
  395.4 0.7 select_maximum_fusion.4
  396.1 0.7 select_maximum_fusion.5
  396.8 2.4 multiply_reduce_fusion.2
  399.3 0.6 copy.36
  399.9 5.1 fusion.51
  404.9 2.0 fusion.52
  406.9 0.7 select_maximum_fusion.4
  407.6 0.7 select_maximum_fusion.5
  408.3 2.4 multiply_reduce_fusion.2
  411.4 14.8 %all-reduce.1 = (f32[512]{0:T(512)}, f32[512]{0:T(512)}) all-reduce(f32[512]{0:T(512)} %get-tuple-element.120, f32[512]{0:T(512)S(1)} %get-tuple-element.118), channel_id=1, replica_groups=mesh['query'=32,'entity'=8] {'entity'}, use_global_device_ids=true, to_apply=%region_12.13 | all-reduce | flops 1024 | bytes 8192 | tf_op jit(solution)/shard_map/pmax | solution.py:86
  426.2 0.7 fusion.24
  426.9 14.5 %all-reduce = (f32[512]{0:T(512)S(1)}, f32[512]{0:T(512)}, f32[512]{0:T(512)}) all-reduce(f32[512]{0:T(512)S(1)} %get-tuple-element.261, f32[512]{0:T(512)S(1)} %get-tuple-element.259, f32[512]{0:T(512)S(1)} %get-tuple-element.258), channel_id=1, replica_groups=mesh['query'=32,'entity'=8] {'entity'}, use_global_device_ids=true, to_apply=%region_13.14 | all-reduce | flops 1536 | bytes 12288 | tf_op jit(solution)/shard_map/psum | solution.py:89
  441.4 26.0 %while.33 = (s32[]{:T(128)}, f32[512,128]{1,0:T(8,128)S(1)}, f32[4,1024,128]{2,1,0:T(8,128)}, bf16[4,1024,128]{2,1,0:T(8,128)(2,1)}, bf16[512,128]{1,0:T(8,128)(...) while((s32[]{:T(128)}, f32[512,128]{1,0:T(8,128)S(1)}, ...), condition=%wide.region_15.16_spmd.clone, body=%wide.region_14.15_spmd.clone.sunk | while | flops 1454505984 | bytes 16531671 | solution.py:106
  441.4 3.2 fusion.62
  444.6 1.5 subtract_convert_fusion.4
  446.6 1.2 fusion.63
  447.9 3.2 fusion.62
  451.1 1.5 subtract_convert_fusion.4
  453.1 1.2 fusion.63
  454.4 3.2 fusion.62
  457.6 1.5 subtract_convert_fusion.4
  459.6 1.2 fusion.63
  460.9 3.2 fusion.62
  464.1 1.5 subtract_convert_fusion.4
  466.1 1.2 fusion.63
  467.4 0.7 copy-done.2
  468.7 1.3 log_add_fusion
  469.9 69.6 %all-reduce.6.cloned.1.call-done = f32[512,128]{1,0:T(8,128)} async-done(((f32[512,128]{1,0:T(8,128)}), f32[512,128]{1,0:T(8,128)}) %all-reduce.6.cloned.1.call-update) | async-done | bytes 262160 | tf_op jit(solution)/shard_map/psum | solution.py:109
  539.5 233.4 %reduce-scatter.2.cloned.1.call-done = f32[128,128]{1,0:T(8,128)} async-done(((f32[4096,128]{1,0:T(8,128)}), f32[128,128]{1,0:T(8,128)}) %reduce-scatter.2.cloned.1.call-update) | async-done | bytes 65552 | tf_op jit(solution)/shard_map/reduce_scatter | solution.py:108
  772.9 1.7 copy.48
  (127 shorter events, 4.3 us)
Async XLA Ops:
  7.2 306.7 %copy-start = (bf16[4131,128]{1,0:T(8,128)(2,1)S(1)}, bf16[4131,128]{1,0:T(8,128)(2,1)}, u32[]{:S(2)}) copy-start(bf16[4131,128]{1,0:T(8,128)(2,1)} %param.17) | copy-start | bytes 3172612
  12.4 14.1 %copy-start.15 = (s32[512]{0:T(512)S(1)}, s32[512]{0:T(512)}, u32[]{:S(2)}) copy-start(s32[512]{0:T(512)} %param.11) | copy-start | bytes 6148
  12.4 260.9 %all-to-all-start = ((bf16[32,128,1000]{1,2,0:T(8,128)(2,1)}), bf16[32,128,1000]{1,2,0:T(8,128)(2,1)}, u32[]{:S(2)}, u32[]{:S(2)}) async-start(bf16[32,128,1000]{1,2,0:T(8,128)(2,1)} %stack.2), calls=%async_computation | async-start | bytes 16384000 | tf_op jit(solution)/shard_map/all_to_all | solution.py:7
  25.7 244.3 %all-gather.2.cloned.1.call-start = ((), (), s32[]{:S(2)}) async-start(), calls=%async_computation.2 | async-start | bytes 1081344 | tf_op jit(solution)/shard_map/all_gather | solution.py:37
  26.5 334.6 %all-reduce.8.cloned.1.call-start = ((), (), s32[]{:S(2)}) async-start(), calls=%async_computation.5 | async-start | bytes 2359296 | tf_op jit(solution)/shard_map/psum | solution.py:47
  291.9 1.6 copy-start.13
  293.2 246.3 %all-reduce.6.cloned.1.call-start = ((), (), s32[]{:S(2)}) async-start(), calls=%async_computation.4 | async-start | bytes 524288 | tf_op jit(solution)/shard_map/psum | solution.py:109
  305.8 9.4 %copy-start.14 = (s32[512]{0:T(512)S(1)}, s32[512]{0:T(512)}, u32[]{:S(2)}) copy-start(s32[512]{0:T(512)} %param.13) | copy-start | bytes 6148
  361.1 1.5 copy-start.5
  361.1 1.5 copy-start.12
  363.6 1.3 copy-start.3
  373.8 2.4 copy-start.4
  373.8 2.4 copy-start.6
  373.8 2.4 copy-start.8
  373.8 2.4 copy-start.10
  376.2 0.6 copy-start.7
  376.2 0.6 copy-start.9
  376.3 0.6 copy-start.11
  385.3 2.4 copy-start.4
  385.3 2.4 copy-start.6
  385.3 2.4 copy-start.8
  385.3 2.4 copy-start.10
  387.7 0.6 copy-start.7
  387.8 0.6 copy-start.9
  387.8 0.6 copy-start.11
  396.8 2.4 copy-start.4
  396.8 2.4 copy-start.6
  396.8 2.4 copy-start.8
  396.8 2.4 copy-start.10
  399.2 0.6 copy-start.7
  399.3 0.6 copy-start.9
  399.3 0.6 copy-start.11
  408.3 2.4 copy-start.4
  408.3 2.4 copy-start.6
  408.3 2.4 copy-start.8
  408.3 2.4 copy-start.10
  410.7 0.6 copy-start.7
  410.8 0.6 copy-start.9
  410.8 0.6 copy-start.11
  441.4 3.2 copy-start.1
  441.4 3.2 copy-start.16
  447.9 3.2 copy-start.1
  447.9 3.2 copy-start.16
  454.4 3.2 copy-start.1
  454.4 3.2 copy-start.16
  460.9 3.2 copy-start.1
  460.9 3.2 copy-start.16
  467.4 0.7 copy-start.2
  467.4 1.3 copy-start.17
  467.4 1.3 copy-start.18
  468.1 304.9 %reduce-scatter.2.cloned.1.call-start = ((), (), s32[]{:S(2)}) async-start(), calls=%async_computation.3 | async-start | bytes 2162688 | tf_op jit(solution)/shard_map/reduce_scatter | solution.py:108
Sparse Core Ops, SparseCore 0:
  30.0 240.0 all-gather.1
  293.3 67.7 all-reduce.7
  468.2 71.2 all-reduce.5
  542.6 230.2 reduce-scatter.1
